TPU v7x, 32 devices: a whole 2x2x4 slice. The times are simulated.
32 devices in a mesh: dp: 8 (over z, core), expert: 4 (over y, x).
Axes of the slice: x: 2, y: 2, z: 4, core: 2. Of those that a mesh axis runs over, the one named last changes fastest.
Arguments:
- tokens: bfloat16 [6144, 4096], P(('dp', 'expert')), may hold values from -24 to 24
- routes: int32 [6144, 2], P(('dp', 'expert')), may hold values from 0 to 3, all different within a row; in each aligned block of 192 rows (0 to 191, 192 to 383, ...) at most 128 rows name the same one
- positives: int32 [64], P(('dp', 'expert')), may hold values from 0 to 63, each once
- expert_out: bfloat16 [8, 4, 4, 128, 4096], P('dp', 'expert'), may hold values from -6 to 6
- router: bfloat16 [4096, 4], replicated, may hold values from -0.09375 to 0.09375
- norm_gain: float32 [4096], replicated, may hold values from 0.25 to 1.75
- loss_scale: float32 [], replicated, may hold values from 8192 to 65536
Outputs:
- token_grad: bfloat16 [6144, 4096], P(('dp', 'expert'))
- expert_grad: bfloat16 [8, 4, 4, 128, 4096], P('dp', 'expert')
- router_grad: float32 [4096, 4], replicated
- loss: float32 [], replicated
Inputs may be any that keep to these rules, and one draw needn't show every extreme that they name: `routes`: each row names 2 different experts; among the rows of one device no expert is named by more than 128 rows, a bound that some block reaches. `positives`: A permutation of the records.
All inputs are finite; a program needn't handle non-finite values.
Results may differ from a plain program's by a relative error of at most 0.0061.
Values may be sent and summed in bfloat16 or wider, within the bound.
A program may use at most 128 MiB of HBM per device.

v0:
```python
import math

import jax
import jax.numpy as jnp
from jax import lax
from jax.sharding import PartitionSpec as P

PAIR_DEV = 2
SEQ = 48


norm_eps = 1e-05


def slot_where(routes, experts, capacity):
    hit_table = (routes[:, :, None] == jnp.arange(experts, dtype=jnp.int32)[None, None, :]).astype(
        jnp.int32
    )
    flat_hits = hit_table.reshape(-1, experts)
    before = jnp.cumsum(flat_hits, axis=0) - flat_hits
    slot_rank = jnp.sum(before * flat_hits, axis=1).reshape(routes.shape)
    return routes * capacity + slot_rank


def forward_rows(tokens, routes, received, router, norm_gain):
    experts = received.shape[0]
    capacity = received.shape[1]
    hidden_width = received.shape[2]
    logits = jnp.dot(tokens, router, preferred_element_type=jnp.float32)
    one_hot = (routes[:, :, None] == jnp.arange(experts, dtype=jnp.int32)[None, None, :]).astype(
        jnp.float32
    )
    chosen = jnp.sum(one_hot * logits[:, None, :], axis=2)
    gate_mix = jax.nn.softmax(chosen, axis=1)
    slot_rows = slot_where(routes, experts, capacity)
    fetched = received.reshape(experts * capacity, hidden_width)[slot_rows]
    summed_rows = (
        tokens.astype(jnp.float32)
        + gate_mix[:, 0:1] * fetched[:, 0].astype(jnp.float32)
        + gate_mix[:, 1:2] * fetched[:, 1].astype(jnp.float32)
    )
    inverse = lax.rsqrt(jnp.mean(summed_rows * summed_rows, axis=1, keepdims=True) + norm_eps)
    normed = summed_rows * inverse * norm_gain
    pooled = jnp.mean(normed.reshape(-1, SEQ, hidden_width), axis=1).astype(jnp.bfloat16)
    return (pooled, (gate_mix, one_hot, slot_rows, fetched, summed_rows, inverse))


def backward_rows(tokens, router, norm_gain, saved, grad_pool, experts, capacity):
    gate_mix, one_hot, slot_rows, fetched, summed_rows, inverse = saved
    hidden_width = tokens.shape[1]
    grad_rows = jnp.broadcast_to(
        grad_pool[:, None, :] / SEQ, (grad_pool.shape[0], SEQ, hidden_width)
    ).reshape(-1, hidden_width)
    weighted = grad_rows * norm_gain
    grad_summed = inverse * weighted - summed_rows * inverse**3 * jnp.mean(
        weighted * summed_rows, axis=1, keepdims=True
    )
    grad_gate = jnp.sum(grad_summed[:, None, :] * fetched.astype(jnp.float32), axis=2)
    grad_chosen = gate_mix * (grad_gate - jnp.sum(gate_mix * grad_gate, axis=1, keepdims=True))
    grad_logits = jnp.sum(one_hot * grad_chosen[:, :, None], axis=1).astype(jnp.bfloat16)
    router_part = lax.dot_general(
        tokens, grad_logits, (((0,), (0,)), ((), ())), preferred_element_type=jnp.float32
    )
    through_router = lax.dot_general(
        grad_logits, router, (((1,), (1,)), ((), ())), preferred_element_type=jnp.float32
    )
    token_grad = (grad_summed + through_router).astype(jnp.bfloat16)
    outgoing = (
        (gate_mix[:, :, None] * grad_summed[:, None, :])
        .astype(jnp.bfloat16)
        .reshape(-1, hidden_width)
    )
    sendback = (
        jnp.zeros((experts * capacity, hidden_width), jnp.bfloat16)
        .at[slot_rows.reshape(-1)]
        .set(outgoing)
    )
    return (token_grad, sendback.reshape(experts, capacity, hidden_width), router_part)


def score_rows(queries, records_all, positives, loss_scale, pair_total, score_scale):
    scores = (
        lax.dot_general(
            queries, records_all, (((1,), (1,)), ((), ())), preferred_element_type=jnp.float32
        )
        * score_scale
    )
    highest = jnp.max(scores, axis=1, keepdims=True)
    log_total = highest[:, 0] + jnp.log(jnp.sum(jnp.exp(scores - highest), axis=1))
    is_positive = jnp.arange(pair_total, dtype=jnp.int32)[None, :] == positives[:, None]
    positive_score = jnp.sum(jnp.where(is_positive, scores, jnp.zeros_like(scores)), axis=1)
    row_loss = log_total - positive_score
    softmax_rows = jnp.exp(scores - log_total[:, None])
    score_grad = (
        (softmax_rows - is_positive.astype(jnp.float32)) * (loss_scale / pair_total)
    ).astype(jnp.bfloat16)
    return (row_loss, score_grad)


def shards(tokens, routes, positives, expert_out, router, norm_gain, loss_scale):
    experts = expert_out.shape[2]
    capacity = expert_out.shape[3]
    hidden_width = expert_out.shape[4]
    received = lax.all_to_all(
        expert_out.reshape(experts, capacity, hidden_width),
        "expert",
        split_axis=0,
        concat_axis=0,
        tiled=True,
    )
    pooled, saved = forward_rows(tokens, routes, received, router, norm_gain)
    queries = pooled[:PAIR_DEV]
    records = pooled[PAIR_DEV:]
    loop_size = lax.axis_size("dp")
    column_size = lax.axis_size("expert")
    device_count = loop_size * column_size
    pair_total = PAIR_DEV * device_count
    score_scale = 4.0 / math.sqrt(hidden_width)
    records_all = lax.all_gather(records, ("dp", "expert"), axis=0, tiled=True)
    row_loss, score_grad = score_rows(
        queries, records_all, positives, loss_scale, pair_total, score_scale
    )
    loss_local = jnp.sum(row_loss)
    grad_queries = (
        jnp.dot(score_grad, records_all, preferred_element_type=jnp.float32) * score_scale
    )
    grad_records = lax.psum_scatter(
        lax.dot_general(
            score_grad, queries, (((0,), (0,)), ((), ())), preferred_element_type=jnp.float32
        )
        * score_scale,
        ("dp", "expert"),
        scatter_dimension=0,
        tiled=True,
    )
    grad_pool = jnp.concatenate([grad_queries, grad_records], axis=0)
    token_grad, sendback, router_part = backward_rows(
        tokens, router, norm_gain, saved, grad_pool, experts, capacity
    )
    returned = lax.all_to_all(sendback, "expert", split_axis=0, concat_axis=0, tiled=True)
    router_grad, loss_total = lax.psum((router_part, loss_local), ("dp", "expert"))
    expert_grad = returned.reshape(1, 1, experts, capacity, hidden_width)
    return (token_grad, expert_grad, router_grad, loss_total / pair_total)


def solution(mesh):
    placed = (
        P(("dp", "expert"), None),
        P(("dp", "expert"), None),
        P(("dp", "expert")),
        P("dp", "expert", None, None, None),
        P(),
        P(),
        P(),
    )
    return jax.shard_map(
        shards,
        mesh=mesh,
        in_specs=placed,
        out_specs=(P(("dp", "expert"), None), P("dp", "expert", None, None, None), P(), P()),
        check_vma=False,
    )
```

profile of v0, /device:TPU:0, one launch (start us, length us, event | category | flops | bytes accessed | tf_op | source)
XLA Modules:
  0.0 551.1 jit_solution(1914578303000155300)
XLA Ops:
  7.2 5.3 all-to-all-start
  12.5 0.1 copy.45
  12.6 0.1 eq.59
  12.8 0.1 eq.55
  12.9 1.2 reduce-window.6
  14.2 0.2 slice_reduce_fusion
  14.4 0.2 reduce-window.9
  14.7 0.1 reshape.211
  14.9 0.1 copy.48
  15.0 0.1 reshape.221
  15.9 0.5 fusion.21
  16.5 44.6 %all-to-all-done = bf16[4,128,4096]{2,1,0:T(8,128)(2,1)} async-done(((bf16[4,128,4096]{2,1,0:T(8,128)(2,1)}), bf16[4,128,4096]{2,1,0:T(8,128)(2,1)}, u32[]{:S(2)}, u32[]{:S(2)}) %all-to-all-start) | async-done | bytes 4194336 | tf_op jit(solution)/shard_map/all_to_all | solution.py:104
  61.1 11.0 %gather_fusion = bf16[384,4096]{1,0:T(8,128)(2,1)} fusion(bf16[512,4096]{1,0:T(8,128)(2,1)} %bitcast.2, s32[1024]{0:T(1024)S(1)} %pad_clamp_fusion), kind=kCustom, calls=%fused_computation | custom fusion | bytes 6292992 | tf_op jit(solution)/shard_map/gather | solution.py:36
  72.1 4.6 reshape.220
  76.7 7.0 %fusion.18 = (bf16[192,1,4096]{2,1,0:T(2,128)(2,1)S(1)}, bf16[192,1,4096]{2,1,0:T(2,128)(2,1)S(1)}) fusion(bf16[192,2,4096]{2,1,0:T(2,128)(2,1)S(1)} %reshape.220), kind=kLoop, calls=%fused_computation.63 | loop fusion | bytes 6291456 | tf_op jit(solution)/shard_map/slice | solution.py:39
  83.7 4.0 multiply_reduce_fusion.2
  87.8 2.4 multiply_multiply_fusion
  90.2 0.3 copy-done.2
  90.5 2.2 reduce_sum.112
  92.7 74.6 %all-gather = bf16[32,2,4096]{2,1,0:T(2,128)(2,1)} all-gather(bf16[1,2,4096]{2,1,0:T(2,128)(2,1)S(1)} %slice_bitcast_fusion), channel_id=1, replica_groups=mesh['dp'=8,'expert'=4] {'dp','expert'}, dimensions={0}, use_global_device_ids=true | all-gather | bytes 540672 | tf_op jit(solution)/shard_map/all_gather | solution.py:119
  167.3 2.1 reshape.238
  169.3 1.4 fusion.20
  170.7 0.2 select_reduce_fusion.2
  171.0 0.6 subtract_reduce_fusion
  171.6 1.4 convolution_multiply_fusion
  173.0 0.1 copy.54
  173.1 0.1 copy.53
  173.3 0.1 reshape.214
  173.4 0.1 div.48
  173.6 1.4 convolution_multiply_fusion.1
  174.9 124.0 %all-reduce.6.cloned.1.call-done = f32[64,4096]{1,0:T(8,128)} async-done(((f32[64,4096]{1,0:T(8,128)}), f32[64,4096]{1,0:T(8,128)}) %all-reduce.6.cloned.1.call-update) | async-done | bytes 1048592
  299.0 1.1 constant_dynamic-slice_fusion
  300.1 0.3 bitcast_multiply_fusion
  300.4 0.5 copy-done.3
  300.9 0.4 multiply_reduce_fusion.1
  301.3 0.7 multiply_subtract_fusion
  302.0 1.7 copy-done.1
  303.7 5.3 mul.182
  309.0 8.4 %mul.189 = f32[384,4096]{1,0:T(8,128)} reshape(f32[192,2,4096]{2,1,0:T(2,128)} %mul.182) | data formatting | bytes 12582912 | tf_op jit(solution)/shard_map/mul | solution.py:58
  317.4 9.7 %scatter_custom_fusion = bf16[512,4096]{1,0:T(8,128)(2,1)} fusion(s32[384]{0:T(512)S(1)} %fusion.12, f32[384,4096]{1,0:T(8,128)} %mul.189, f32[384]{0:T(512)S(1)} %div.48, bf16[]{:T(256)} %constant.41.clone.1), kind=kCustom, calls=%fused_computation.9 | custom fusion | flops 3145728 | bytes 10487810 | tf_op jit(solution)/shard_map/scatter | solution.py:76
  327.1 4.9 all-to-all-start.1
  332.0 79.2 %psum.15 = f32[]{:T(128)} all-reduce(f32[]{:T(128)} %get-tuple-element.6), channel_id=1, replica_groups=mesh['dp'=8,'expert'=4] {'dp','expert'}, use_global_device_ids=true, to_apply=%region_19.20 | all-reduce | flops 1 | bytes 8 | tf_op jit(solution)/shard_map/psum | solution.py:141
  411.9 5.7 %multiply_reduce_fusion = f32[192,2]{1,0:T(8,128)S(1)} fusion(bf16[192,2,4096]{2,1,0:T(2,128)(2,1)S(1)} %reshape.220, f32[192,4096]{1,0:T(8,128)} %copy-done.1), kind=kLoop, calls=%fused_computation.3 | loop fusion | flops 4718208 | bytes 6292992 | tf_op jit(solution)/shard_map/reduce_sum | solution.py:58
  417.8 2.4 convolution_bitcast_fusion
  420.1 3.7 fusion
  423.8 114.0 %all-reduce.4.cloned.1.call-done = f32[4096,4]{0,1:T(4,128)} async-done(((f32[4096,4]{0,1:T(4,128)}), f32[4096,4]{0,1:T(4,128)}) %all-reduce.4.cloned.1.call-update) | async-done | bytes 65552 | tf_op jit(solution)/shard_map/psum | solution.py:141
  537.8 4.7 copy.71
  542.5 0.6 copy.72
  (43 shorter events, 0.7 us)
Async XLA Ops:
  7.2 8.7 %copy-start = (bf16[4096,4]{0,1:T(4,128)(2,1)S(1)}, bf16[4096,4]{0,1:T(4,128)(2,1)}, u32[]{:S(2)}) copy-start(bf16[4096,4]{0,1:T(4,128)(2,1)} %param.11) | copy-start | bytes 98308
  7.2 5.3 copy-start.8
  7.2 8.7 %copy-start.4 = (bf16[192,4096]{1,0:T(8,128)(2,1)S(1)}, bf16[192,4096]{1,0:T(8,128)(2,1)}, u32[]{:S(2)}) copy-start(bf16[192,4096]{1,0:T(8,128)(2,1)} %param.7) | copy-start | bytes 4718596
  7.2 53.9 %all-to-all-start = ((bf16[4,128,4096]{2,1,0:T(8,128)(2,1)}), bf16[4,128,4096]{2,1,0:T(8,128)(2,1)}, u32[]{:S(2)}, u32[]{:S(2)}) async-start(bf16[4,128,4096]{2,1,0:T(8,128)(2,1)} %bitcast.56), calls=%async_computation | async-start | bytes 8388608 | tf_op jit(solution)/shard_map/all_to_all | solution.py:104
  12.5 286.4 %all-reduce.6.cloned.1.call-start = ((), (), s32[]{:S(2)}) async-start(), calls=%async_computation.3 | async-start | bytes 2097152
  76.7 7.0 %copy-start.5 = (bf16[192,4096]{1,0:T(8,128)(2,1)S(1)}, bf16[192,4096]{1,0:T(8,128)(2,1)}, u32[]{:S(2)}) copy-start(bf16[192,4096]{1,0:T(8,128)(2,1)} %param.7) | copy-start | bytes 4718596
  83.7 4.1 copy-start.6
  87.8 2.7 copy-start.2
  90.5 80.3 %copy-start.9 = (s32[2]{0:T(128)S(1)}, s32[2]{0:T(128)}, u32[]{:S(2)}) copy-start(s32[2]{0:T(128)} %param.9) | copy-start | bytes 28
  299.0 2.0 copy-start.3
  302.0 1.7 copy-start.1
  327.1 96.7 %all-to-all-start.1 = ((bf16[4,128,4096]{2,1,0:T(8,128)(2,1)}), bf16[4,128,4096]{2,1,0:T(8,128)(2,1)}, u32[]{:S(2)}, u32[]{:S(2)}) async-start(bf16[4,128,4096]{2,1,0:T(8,128)(2,1)} %bitcast.54), calls=%async_computation.1 | async-start | bytes 8388608 | tf_op jit(solution)/shard_map/all_to_all | solution.py:140
  332.0 205.8 %all-reduce.4.cloned.1.call-start = ((), (), s32[]{:S(2)}) async-start(), calls=%async_computation.2 | async-start | bytes 131072 | tf_op jit(solution)/shard_map/psum | solution.py:141
  537.7 4.7 copy-start.7
Sparse Core Ops, SparseCore 0:
  173.1 125.7 all-reduce.5
  420.3 117.4 all-reduce.3
where the time goes:
time: 553 us; the launch traced here: 551 us
  waiting for transfers between devices  283 us (51%)
  blocking collectives  154 us (28%)
  local copies, waits for them, and re-layouts  49 us (9%)
  other arithmetic  28 us (5%)
  between operations  16.8 us (3%)
  matrix products  10.7 us (2%)
  starting transfers between devices  10.2 us (2%)
    unnamed x3, waiting for transfers between devices  124 us
    psum x1, waiting for transfers between devices, shards(): lax.psum((router_part, loss_local), ('dp', 'expert'))  114 us
    psum x1, blocking collectives, shards(): lax.psum((router_part, loss_local), ('dp', 'expert'))  79.2 us
    all_gather x1, blocking collectives, shards(): records_all = lax.all_gather(records, ('dp', 'expert'), axis=0, tiled=True)  74.6 us
    all_to_all x1, waiting for transfers between devices, shards(): lax.all_to_all(expert_out.reshape(experts, capacity, hidden_width), 'expe...  44.6 us
    gather x2, local copies, waits for them, and re-layouts, forward_rows(): fetched = received.reshape(experts * capacity, hidden_width)[slot_rows]  15.5 us
    mul x2, local copies, waits for them, and re-layouts, backward_rows(): grad_summed[:, None, :] * fetched.astype(jnp.float32)  13.8 us
    unnamed x26, local copies, waits for them, and re-layouts  11.1 us
  transfers between devices with their start and end apart: 4, of which 3 were waited for; matrix products, arithmetic and copies ran while one was open for 3% of the time, Pallas kernels for 0%

commit v1 on v0

v1 whole, which is shorter than its diff:
```python
import functools
import math

import jax
import jax.numpy as jnp
from jax import lax
from jax.experimental import pallas as pl
from jax.experimental.pallas import tpu as pltpu
from jax.sharding import PartitionSpec as P

PAIR_DEV = 2
SEQ = 48
NORM_EPS = 1e-05
CHUNKS = 4
TILE = 512
MESH = pl.DeviceIdType.MESH
BF16, F32, I32 = jnp.bfloat16, jnp.float32, jnp.int32
NT = (((1,), (1,)), ((), ()))


def iota(shape, dim):
    return lax.broadcasted_iota(I32, shape, dim)


def dot(a, b):
    return jnp.dot(a, b, preferred_element_type=F32)


def dot_nt(a, b):
    return lax.dot_general(a, b, NT, preferred_element_type=F32)


def lane_sum(x):
    return jnp.sum(x, axis=1, keepdims=True)


def fold(x):
    total = x[:, :128]
    for i in range(1, x.shape[1] // 128):
        total = total + x[:, i * 128 : (i + 1) * 128]
    return total


def split3(x):
    hi = x.astype(BF16).astype(F32)
    mid = (x - hi).astype(BF16).astype(F32)
    return hi, mid, x - hi - mid


def log2(n):
    assert n & (n - 1) == 0
    return n.bit_length() - 1


def kernel(
    n_dp, n_ep, experts, cap,
    tok_hbm, routes_ref, pos_ref, eo_hbm, router_ref, gain_ref, scale_ref,
    tg_hbm, eg_hbm, rg_out, loss_ref,
    tok, recv, feat, summed, sq, sf, pick, pick_t, back, xrows, pay, gath, qr, ghl, tgb, rpart, rsb, exb, agb,
    tok_sem, own_sem, a_send, a_recv, z_send, z_recv, e_send, e_recv, c_send, c_recv,
    b_send, b_recv, r_send, r_recv, x_send, x_recv, g_send, g_recv, out_sem,
):
    d = lax.axis_index("dp")
    e = lax.axis_index("expert")
    rows, width = tok.shape
    slots = experts * cap
    n_z = n_dp // 2
    core, z = lax.rem(d, 2), d // 2
    pairs = PAIR_DEV * n_dp * n_ep
    wc = width // CHUNKS
    wr = width // n_dp
    ng = PAIR_DEV * n_ep
    score_scale = 4.0 / math.sqrt(width)

    def dp_peer(o):
        return lax.rem(d + o, n_dp)

    def ep_peer(o):
        return lax.rem(e + o, n_ep)

    barrier = pltpu.get_barrier_semaphore()
    for o in range(1, n_dp):
        pl.semaphore_signal(barrier, inc=1, device_id=(dp_peer(o), e), device_id_type=MESH)
    for o in range(1, n_ep):
        pl.semaphore_signal(barrier, inc=1, device_id=(d, ep_peer(o)), device_id_type=MESH)

    tok_copy = pltpu.make_async_copy(tok_hbm, tok, tok_sem.at[0])
    tok_copy.start()

    def ep_rows(i):
        return pl.ds(pl.multiple_of(i * cap, cap), cap)

    own_copy = pltpu.make_async_copy(eo_hbm.at[ep_rows(e)], recv.at[ep_rows(e)], own_sem.at[0])
    own_copy.start()
    pl.semaphore_wait(barrier, n_dp - 1 + n_ep - 1)

    a_copies = []
    for c in range(CHUNKS):
        cols = pl.ds(c * wc, wc)
        for o in range(1, n_ep):
            copy = pltpu.make_async_remote_copy(
                src_ref=eo_hbm.at[ep_rows(ep_peer(o)), cols],
                dst_ref=recv.at[ep_rows(e), cols],
                send_sem=a_send.at[c, o - 1],
                recv_sem=a_recv.at[c, o - 1],
                device_id=(d, ep_peer(o)),
                device_id_type=MESH,
            )
            copy.start()
            a_copies.append(copy)

    tok_copy.wait()
    logits = dot_nt(tok[...], router_ref[...])
    route = [routes_ref[:, 0:1], routes_ref[:, 1:2]]
    lane_e = iota((rows, 128), 1)
    lane_l = iota(logits.shape, 1)
    chosen = [lane_sum(jnp.where(lane_l == r, logits, 0.0)) for r in route]
    highest = jnp.maximum(chosen[0], chosen[1])
    expo = [jnp.exp(x - highest) for x in chosen]
    gate = [x / (expo[0] + expo[1]) for x in expo]
    hits = jnp.where((lane_e == route[0]) | (lane_e == route[1]), 1.0, 0.0).astype(BF16)
    lower = jnp.where(iota((rows, rows), 1) < iota((rows, rows), 0), 1.0, 0.0).astype(BF16)
    before = dot(lower, hits)
    column = iota((rows, slots), 1).astype(F32)
    for k in range(2):
        rank = lane_sum(jnp.where(lane_e == route[k], before, 0.0))
        slot = route[k].astype(F32) * float(cap) + rank
        one = jnp.where(column == slot, 1.0, 0.0)
        pick[k * rows : (k + 1) * rows, :] = one.astype(BF16)
        pick_t[k, :, :] = jnp.transpose(one).astype(BF16)

    sq[...] = jnp.zeros_like(sq)
    sf[...] = jnp.zeros_like(sf)
    own_copy.wait()
    for c in range(CHUNKS):
        for o in range(1, n_ep):
            a_copies[c * (n_ep - 1) + o - 1].wait_recv()

        def forward(i, _, c=c):
            cols = pl.ds(pl.multiple_of(c * wc + i * TILE, TILE), TILE)
            got = dot(pick[...], recv[:, cols])
            feat[:, cols] = got.astype(BF16)
            f0, f1 = got[:rows], got[rows:]
            s = tok[:, cols].astype(F32) + gate[0] * f0 + gate[1] * f1
            summed[:, cols] = s
            sq[...] += fold(s * s)
            sf[0, :, :] += fold(s * f0)
            sf[1, :, :] += fold(s * f1)
            return 0

        lax.fori_loop(0, wc // TILE, forward, 0)

    inverse = lax.rsqrt(lane_sum(sq[...]) * (1.0 / width) + NORM_EPS)
    for c in range(CHUNKS):
        for i in range(wc // TILE):
            cols = slice(c * wc + i * TILE, c * wc + (i + 1) * TILE)
            normed = summed[:, cols] * inverse * gain_ref[:, cols]
            for q in range(2 * PAIR_DEV):
                pay[c * 4 + q : c * 4 + q + 1, i * TILE : (i + 1) * TILE] = jnp.sum(
                    normed[q * SEQ : (q + 1) * SEQ], axis=0, keepdims=True
                ) * (1.0 / SEQ)
    tag_row, tag_lane = iota((16, 128), 0), iota((16, 128), 1)
    tags = jnp.zeros((16, 128), F32)
    for q in range(PAIR_DEV):
        p = pos_ref[q]
        high = jnp.right_shift(p, 4).astype(F32)
        low = jnp.bitwise_and(p, 15).astype(F32)
        tags = jnp.where((tag_row == q) & (tag_lane == 0), high, tags)
        tags = jnp.where((tag_row == q) & (tag_lane == 1), low, tags)
    pay[:, wc:] = tags

    def block(first, count):
        return pl.ds(pl.multiple_of(first * 16, 16), count * 16)

    mine = (core * n_ep + e) * n_z + z
    gath[block(mine, 1), :] = pay[...].astype(BF16)
    z_copies = []
    for o in range(1, n_z):
        copy = pltpu.make_async_remote_copy(
            src_ref=gath.at[block(mine, 1)],
            dst_ref=gath.at[block(mine, 1)],
            send_sem=z_send.at[o - 1],
            recv_sem=z_recv.at[o - 1],
            device_id=(dp_peer(2 * o), e),
            device_id_type=MESH,
        )
        copy.start()
        z_copies.append(copy)

    seq_of = iota((rows, 1), 0) // SEQ
    code = jnp.where(seq_of < PAIR_DEV, e * PAIR_DEV + seq_of, ng + e * PAIR_DEV + seq_of - PAIR_DEV)
    inv3 = split3(inverse)
    notes = jnp.zeros((slots, 128), F32)
    for k in range(2):
        values = list(split3(gate[k])) + list(inv3) + [code.astype(F32)]
        note = jnp.zeros((rows, 128), F32)
        for i, v in enumerate(values):
            note = jnp.where(lane_e == i, v, note)
        notes = notes + dot(pick_t[k], note.astype(BF16))
    back[:, width:] = notes.astype(BF16)

    def place(i, _):
        cols = pl.ds(pl.multiple_of(i * TILE, TILE), TILE)
        both = pick_t[0] + pick_t[1]
        back[:, cols] = dot(both, summed[:, cols].astype(BF16)).astype(BF16)
        return 0

    lax.fori_loop(0, width // TILE, place, 0)

    for copy in z_copies:
        copy.wait_recv()
    line = (core * n_ep + e) * n_z
    e_copies = []
    for o in range(1, n_ep):
        copy = pltpu.make_async_remote_copy(
            src_ref=gath.at[block(line, n_z)],
            dst_ref=gath.at[block(line, n_z)],
            send_sem=e_send.at[o - 1],
            recv_sem=e_recv.at[o - 1],
            device_id=(d, ep_peer(o)),
            device_id_type=MESH,
        )
        copy.start()
        e_copies.append(copy)
    back_own = pltpu.make_async_copy(back.at[ep_rows(e)], xrows.at[ep_rows(e)], own_sem.at[1])
    back_own.start()
    b_copies = []
    for c in range(CHUNKS):
        cols = pl.ds(c * wc, wc + (128 if c == CHUNKS - 1 else 0))
        for o in range(1, n_ep):
            copy = pltpu.make_async_remote_copy(
                src_ref=back.at[ep_rows(ep_peer(o)), cols],
                dst_ref=xrows.at[ep_rows(e), cols],
                send_sem=b_send.at[c, o - 1],
                recv_sem=b_recv.at[c, o - 1],
                device_id=(d, ep_peer(o)),
                device_id_type=MESH,
            )
            copy.start()
            b_copies.append(copy)
    for copy in e_copies:
        copy.wait_recv()
    half = core * n_ep * n_z
    c_copy = pltpu.make_async_remote_copy(
        src_ref=gath.at[block(half, n_ep * n_z)],
        dst_ref=gath.at[block(half, n_ep * n_z)],
        send_sem=c_send.at[0],
        recv_sem=c_recv.at[0],
        device_id=(d + 1 - 2 * core, e),
        device_id_type=MESH,
    )
    c_copy.start()
    c_copy.wait_recv()

    total = n_dp * n_ep * 16
    which = iota((2 * pairs, total), 0)
    source = iota((2 * pairs, total), 1)
    pair = jnp.bitwise_and(which, pairs - 1)
    is_record = jnp.right_shift(which, log2(pairs))
    blk = jnp.right_shift(pair, log2(PAIR_DEV))
    of_e = jnp.bitwise_and(blk, n_ep - 1)
    of_d = jnp.right_shift(blk, log2(n_ep))
    place_of = (jnp.bitwise_and(of_d, 1) * n_ep + of_e) * n_z + jnp.right_shift(of_d, 1)
    start = place_of * 16 + is_record * PAIR_DEV + jnp.bitwise_and(pair, PAIR_DEV - 1)
    for c in range(CHUNKS):
        take = jnp.where(source == start + c * 4, 1.0, 0.0).astype(BF16)
        if c == 0:
            tag = dot(take[:pairs], gath[:, wc:])
            positive = tag[:, 0:1] * 16.0 + tag[:, 1:2]
        qr[:, c * wc : (c + 1) * wc] = dot(take, gath[:, :wc]).astype(BF16)
    scores = dot_nt(qr[:pairs], qr[pairs:]) * score_scale
    top = jnp.max(scores, axis=1, keepdims=True)
    log_total = top + jnp.log(lane_sum(jnp.exp(scores - top)))
    is_positive = iota((pairs, pairs), 1).astype(F32) == positive
    positive_score = lane_sum(jnp.where(is_positive, scores, 0.0))
    loss = jnp.sum(log_total - positive_score, axis=0, keepdims=True) * (1.0 / pairs)
    loss_ref[...] = jnp.broadcast_to(loss, loss_ref.shape)
    score_grad = (
        (jnp.exp(scores - log_total) - jnp.where(is_positive, 1.0, 0.0)) * (scale_ref[0] * (1.0 / pairs))
    ).astype(BF16)
    group_shape = (max(16, ng), pairs)
    group = jnp.where(iota(group_shape, 1) == iota(group_shape, 0) + d * ng, 1.0, 0.0).astype(BF16)
    grad_q = dot(group, score_grad).astype(BF16)
    grad_r = dot_nt(group, score_grad).astype(BF16)

    def pooled_grads(i, _):
        cols = pl.ds(pl.multiple_of(i * TILE, TILE), TILE)
        gq = dot(grad_q, qr[pairs:, cols])[:ng]
        gr = dot(grad_r, qr[:pairs, cols])[:ng]
        g = jnp.concatenate([gq, gr], axis=0) * (score_scale / SEQ) * gain_ref[:, cols]
        hi = g.astype(BF16)
        ghl[: 2 * ng, cols] = hi
        ghl[2 * ng :, cols] = (g - hi.astype(F32)).astype(BF16)
        return 0

    lax.fori_loop(0, width // TILE, pooled_grads, 0)

    lane_g = iota((rows, 4 * ng), 1)
    mark = jnp.where((lane_g == code) | (lane_g == code + 2 * ng), 1.0, 0.0)
    own = lane_sum(mark * dot_nt(tok[...], ghl[...]))
    along = dot_nt(feat[...], ghl[...])
    a0, a1 = lane_sum(mark * along[:rows]), lane_sum(mark * along[rows:])
    mean_ws = (own + gate[0] * a0 + gate[1] * a1) * (1.0 / width)
    coef = inverse * inverse * inverse * mean_ws
    gg0 = inverse * a0 - coef * lane_sum(sf[0])
    gg1 = inverse * a1 - coef * lane_sum(sf[1])
    gg = gate[0] * gg0 + gate[1] * gg1
    grad_logits = jnp.where(lane_e == route[0], gate[0] * (gg0 - gg), 0.0) + jnp.where(
        lane_e == route[1], gate[1] * (gg1 - gg), 0.0
    )
    gl = grad_logits[:, :16].astype(BF16)
    gl_t = jnp.transpose(grad_logits)[:16].astype(BF16)
    for i in range(n_dp):
        rpart[i, :, :] = dot(gl_t, tok[:, i * wr : (i + 1) * wr])[:8]
    rsb[d] = rpart[d]
    r_copies = []
    for o in range(1, n_dp):
        copy = pltpu.make_async_remote_copy(
            src_ref=rpart.at[dp_peer(o)],
            dst_ref=rsb.at[d],
            send_sem=r_send.at[o - 1],
            recv_sem=r_recv.at[o - 1],
            device_id=(dp_peer(o), e),
            device_id_type=MESH,
        )
        copy.start()
        r_copies.append(copy)
    markb = mark.astype(BF16)

    def token_grads(i, _):
        cols = pl.ds(pl.multiple_of(i * TILE, TILE), TILE)
        w = dot(markb, ghl[:, cols])
        through = dot(gl, router_ref[:, cols])
        tgb[:, cols] = (inverse * w - coef * summed[:, cols] + through).astype(BF16)
        return 0

    lax.fori_loop(0, width // TILE, token_grads, 0)
    tg_copy = pltpu.make_async_copy(tgb, tg_hbm, out_sem.at[CHUNKS])
    tg_copy.start()

    for copy in r_copies:
        copy.wait_recv()
    part = rsb[0]
    for i in range(1, n_dp):
        part = part + rsb[i]
    exb[e] = part
    x_copies = []
    for o in range(1, n_ep):
        copy = pltpu.make_async_remote_copy(
            src_ref=exb.at[e],
            dst_ref=exb.at[e],
            send_sem=x_send.at[o - 1],
            recv_sem=x_recv.at[o - 1],
            device_id=(d, ep_peer(o)),
            device_id_type=MESH,
        )
        copy.start()
        x_copies.append(copy)

    back_own.wait()
    dots = jnp.zeros((slots, 4 * ng), F32)
    for c in range(CHUNKS):
        for o in range(1, n_ep):
            b_copies[c * (n_ep - 1) + o - 1].wait_recv()
        dots = dots + dot_nt(xrows[:, c * wc : (c + 1) * wc], ghl[:, c * wc : (c + 1) * wc])

    for copy in x_copies:
        copy.wait_recv()
    part = exb[0]
    for i in range(1, n_ep):
        part = part + exb[i]
    agb[d] = part
    g_copies = []
    for o in range(1, n_dp):
        copy = pltpu.make_async_remote_copy(
            src_ref=agb.at[d],
            dst_ref=agb.at[d],
            send_sem=g_send.at[o - 1],
            recv_sem=g_recv.at[o - 1],
            device_id=(dp_peer(o), e),
            device_id_type=MESH,
        )
        copy.start()
        g_copies.append(copy)

    note = xrows[:, width:].astype(F32)
    x_gate = note[:, 0:1] + note[:, 1:2] + note[:, 2:3]
    x_inv = note[:, 3:4] + note[:, 4:5] + note[:, 5:6]
    x_code = note[:, 6:7]
    lane_x = iota((slots, 4 * ng), 1).astype(F32)
    x_mark = jnp.where((lane_x == x_code) | (lane_x == x_code + float(2 * ng)), 1.0, 0.0)
    x_mean = lane_sum(x_mark * dots) * (1.0 / width)
    alpha = x_gate * x_inv
    beta = alpha * x_inv * x_inv * x_mean
    x_markb = x_mark.astype(BF16)
    out_copies = []
    for c in range(CHUNKS):

        def expert_grads(i, _, c=c):
            cols = pl.ds(pl.multiple_of(c * wc + i * TILE, TILE), TILE)
            w = dot(x_markb, ghl[:, cols])
            recv[:, cols] = (alpha * w - beta * xrows[:, cols].astype(F32)).astype(BF16)
            return 0

        lax.fori_loop(0, wc // TILE, expert_grads, 0)
        cols = pl.ds(c * wc, wc)
        copy = pltpu.make_async_copy(recv.at[:, cols], eg_hbm.at[:, cols], out_sem.at[c])
        copy.start()
        out_copies.append(copy)

    for copy in g_copies:
        copy.wait_recv()
    rg_out[...] = agb[...]
    for copy in a_copies + z_copies + e_copies + b_copies + [c_copy] + r_copies + x_copies + g_copies:
        copy.wait_send()
    tg_copy.wait()
    for copy in out_copies:
        copy.wait()


def shards(n_dp, n_ep, tokens, routes, positives, expert_out, router, norm_gain, loss_scale):
    rows, width = tokens.shape
    experts, cap = expert_out.shape[2], expert_out.shape[3]
    slots = experts * cap
    ng = PAIR_DEV * n_ep
    pairs = PAIR_DEV * n_dp * n_ep
    wc, wr = width // CHUNKS, width // n_dp
    dma = pltpu.SemaphoreType.DMA
    vmem = pl.BlockSpec(memory_space=pltpu.VMEM)
    smem = pl.BlockSpec(memory_space=pltpu.SMEM)
    hbm = pl.BlockSpec(memory_space=pl.ANY)
    router_t = jnp.pad(router.T, ((0, 16 - experts), (0, 0)))
    token_grad, expert_grad, router_grad, loss = pl.pallas_call(
        functools.partial(kernel, n_dp, n_ep, experts, cap),
        name="infonce_step",
        out_shape=(
            jax.ShapeDtypeStruct((rows, width), BF16),
            jax.ShapeDtypeStruct((slots, width), BF16),
            jax.ShapeDtypeStruct((n_dp, 8, wr), F32),
            jax.ShapeDtypeStruct((8, 128), F32),
        ),
        in_specs=[hbm, vmem, smem, hbm, vmem, vmem, smem],
        out_specs=(hbm, hbm, vmem, vmem),
        scratch_shapes=[
            pltpu.VMEM((rows, width), BF16),
            pltpu.VMEM((slots, width), BF16),
            pltpu.VMEM((2 * rows, width), BF16),
            pltpu.VMEM((rows, width), F32),
            pltpu.VMEM((rows, 128), F32),
            pltpu.VMEM((2, rows, 128), F32),
            pltpu.VMEM((2 * rows, slots), BF16),
            pltpu.VMEM((2, slots, rows), BF16),
            pltpu.VMEM((slots, width + 128), BF16),
            pltpu.VMEM((slots, width + 128), BF16),
            pltpu.VMEM((16, wc + 128), F32),
            pltpu.VMEM((n_dp * n_ep * 16, wc + 128), BF16),
            pltpu.VMEM((2 * pairs, width), BF16),
            pltpu.VMEM((4 * ng, width), BF16),
            pltpu.VMEM((rows, width), BF16),
            pltpu.VMEM((n_dp, 8, wr), F32),
            pltpu.VMEM((n_dp, 8, wr), F32),
            pltpu.VMEM((n_ep, 8, wr), F32),
            pltpu.VMEM((n_dp, 8, wr), F32),
            dma((1,)),
            dma((2,)),
            dma((CHUNKS, n_ep - 1)),
            dma((CHUNKS, n_ep - 1)),
            dma((n_dp // 2 - 1,)),
            dma((n_dp // 2 - 1,)),
            dma((n_ep - 1,)),
            dma((n_ep - 1,)),
            dma((1,)),
            dma((1,)),
            dma((CHUNKS, n_ep - 1)),
            dma((CHUNKS, n_ep - 1)),
            dma((n_dp - 1,)),
            dma((n_dp - 1,)),
            dma((n_ep - 1,)),
            dma((n_ep - 1,)),
            dma((n_dp - 1,)),
            dma((n_dp - 1,)),
            dma((CHUNKS + 1,)),
        ],
        compiler_params=pltpu.CompilerParams(
            collective_id=0, has_side_effects=True, vmem_limit_bytes=58 * 1024 * 1024
        ),
    )(
        tokens,
        routes,
        positives,
        expert_out.reshape(slots, width),
        router_t,
        norm_gain.reshape(1, width),
        loss_scale.reshape(1),
    )
    router_grad = jnp.transpose(router_grad, (0, 2, 1)).reshape(width, 8)[:, :experts]
    return (token_grad, expert_grad.reshape(expert_out.shape), router_grad, loss[0, 0])


def solution(mesh):
    placed = (
        P(("dp", "expert"), None),
        P(("dp", "expert"), None),
        P(("dp", "expert")),
        P("dp", "expert", None, None, None),
        P(),
        P(),
        P(),
    )
    return jax.shard_map(
        functools.partial(shards, mesh.shape["dp"], mesh.shape["expert"]),
        mesh=mesh,
        in_specs=placed,
        out_specs=(P(("dp", "expert"), None), P("dp", "expert", None, None, None), P(), P()),
        check_vma=False,
    )
```

time: 553 us -> 135 us (0.24)
  waiting for transfers between devices: 283 us -> 0 us
  blocking collectives: 154 us -> 0 us
  Pallas kernels: 0 us -> 121 us
  local copies, waits for them, and re-layouts: 49 us -> 13 us
  other arithmetic: 28 us -> 0 us
  between operations: 16.8 us -> 1.29 us
  matrix products: 10.7 us -> 0 us
  starting transfers between devices: 10.2 us -> 0 us
    unnamed x3 -> x0, waiting for transfers between devices: 124 us -> none
    pallas_call x0 -> x1, Pallas kernels: none -> 121 us  [shards(): pl.pallas_call(functools.partial(kernel, n_dp, n_ep, experts, cap), name=...]
    psum x1 -> x0, waiting for transfers between devices: 114 us -> none  [shards(): lax.psum((router_part, loss_local), ('dp', 'expert'))]
    psum x1 -> x0, blocking collectives: 79.2 us -> none  [shards(): lax.psum((router_part, loss_local), ('dp', 'expert'))]
    all_gather x1 -> x0, blocking collectives: 74.6 us -> none  [shards(): records_all = lax.all_gather(records, ('dp', 'expert'), axis=0, tiled=True)]
    all_to_all x2 -> x0, waiting for transfers between devices: 44.6 us -> none  [the longest x1 44.6 us: shards(): lax.all_to_all(expert_out.reshape(experts, capacity, hidden_width), 'expe...]
    gather x2 -> x0, local copies, waits for them, and re-layouts: 15.5 us -> none  [forward_rows(): fetched = received.reshape(experts * capacity, hidden_width)[slot_rows]]
    mul x2 -> x0, local copies, waits for them, and re-layouts: 13.8 us -> none  [backward_rows(): grad_summed[:, None, :] * fetched.astype(jnp.float32)]
  transfers between devices with their start and end apart: 4 -> 0, of which waited for: 3 -> 0; matrix products, arithmetic and copies ran while one was open for 3% -> 0% of each run, Pallas kernels for 0% -> 0%
where the time goes in v1:
time: 135 us
  Pallas kernels  121 us (90%)
  local copies, waits for them, and re-layouts  13 us (10%)
    pallas_call x1, Pallas kernels, shards(): pl.pallas_call(functools.partial(kernel, n_dp, n_ep, experts, cap), name=...  121 us
    unnamed x3, local copies, waits for them, and re-layouts  8.84 us

profile of v1, /device:TPU:0, one launch (start us, length us, event | category | flops | bytes accessed | tf_op | source)
XLA Modules:
  0.0 134.8 jit_solution(3524240017440524871)
XLA Ops:
  1.3 1.4 %copy.11.routes_ref = s32[192,2]{1,0:T(8,128)} copy(s32[192,2]{0,1:T(2,128)} %param.8) | data formatting | bytes 3072 | tf_op args[1]
  2.7 1.4 %pad.4.router_ref = bf16[16,4096]{1,0:T(8,128)(2,1)} pad(bf16[4,4096]{1,0:T(4,128)(2,1)} %bitcast.12, bf16[]{:T(256)} %constant.2.clone.1), padding=0_12x0_0 | pad | bytes 163842 | tf_op jit(solution)/shard_map/jit(_pad)/pad | solution.py:432
  4.2 120.5 %infonce_step.1 = (bf16[192,4096]{1,0:T(8,128)(2,1)}, bf16[512,4096]{1,0:T(8,128)(2,1)}, f32[8,8,512]{2,1,0:T(8,128)}, f32[8,128]{1,0:T(8,128)}) custom-call(bf16[192,4096]{1,0:T(8,128)(2,1)} %tok_hbm.1, s32[192,2]{1,0:T(8,128)} %copy.11.routes_ref, s32[2]{0:T(128)} %pos_ref.1, bf16[512,4096]{1,0:T(8,128)(2,1)} %bitcast.10, bf16[16,4096]{1,0:T(8,128)(2,1)} %pad.4.router_ref, ...), custom_call_target="tpu_custom_call" | custom-call | tf_op jit(solution)/shard_map/infonce_step/pallas_call | solution.py:433
  124.7 1.2 slice.7
  125.9 1.5 %slice.8 = f32[4096,4]{0,1:T(4,128)} slice(f32[4096,8]{0,1:T(8,128)} %bitcast.13), slice={[0:4096], [0:4]} | slice | bytes 131072 | tf_op jit(solution)/shard_map/slice | solution.py:496
  127.4 2.7 %copy.15 = bf16[192,4096]{1,0:T(8,128)(2,1)} copy(bf16[192,4096]{1,0:T(8,128)(2,1)} %get-tuple-element.16) | data formatting | bytes 3145728
  130.1 4.7 %copy.16 = bf16[1,1,4,128,4096]{4,3,2,1,0:T(8,128)(2,1)} copy(bf16[1,1,4,128,4096]{4,3,2,1,0:T(8,128)(2,1)} %bitcast.11) | data formatting | bytes 8388608

commit v2 on v1

--- a/solution.py
+++ b/solution.py
@@ -55,7 +55,7 @@
 def kernel(
     n_dp, n_ep, experts, cap,
     tok_hbm, routes_ref, pos_ref, eo_hbm, router_ref, gain_ref, scale_ref,
-    tg_hbm, eg_hbm, rg_out, loss_ref,
+    tg_hbm, xr_hbm, rg_out, loss_ref, ghl_out, ab_ref,
     tok, recv, feat, summed, sq, sf, pick, pick_t, back, xrows, pay, gath, qr, ghl, tgb, rpart, rsb, exb, agb,
     tok_sem, own_sem, a_send, a_recv, z_send, z_recv, e_send, e_recv, c_send, c_recv,
     b_send, b_recv, r_send, r_recv, x_send, x_recv, g_send, g_recv, out_sem,
@@ -358,10 +358,16 @@
         x_copies.append(copy)
 
     back_own.wait()
+    ghl_out[...] = ghl[...]
+    out_copies = []
     dots = jnp.zeros((slots, 4 * ng), F32)
     for c in range(CHUNKS):
         for o in range(1, n_ep):
             b_copies[c * (n_ep - 1) + o - 1].wait_recv()
+        cols = pl.ds(c * wc, wc)
+        copy = pltpu.make_async_copy(xrows.at[:, cols], xr_hbm.at[:, cols], out_sem.at[c])
+        copy.start()
+        out_copies.append(copy)
         dots = dots + dot_nt(xrows[:, c * wc : (c + 1) * wc], ghl[:, c * wc : (c + 1) * wc])
 
     for copy in x_copies:
@@ -392,21 +398,10 @@
     x_mean = lane_sum(x_mark * dots) * (1.0 / width)
     alpha = x_gate * x_inv
     beta = alpha * x_inv * x_inv * x_mean
-    x_markb = x_mark.astype(BF16)
-    out_copies = []
-    for c in range(CHUNKS):
-
-        def expert_grads(i, _, c=c):
-            cols = pl.ds(pl.multiple_of(c * wc + i * TILE, TILE), TILE)
-            w = dot(x_markb, ghl[:, cols])
-            recv[:, cols] = (alpha * w - beta * xrows[:, cols].astype(F32)).astype(BF16)
-            return 0
-
-        lax.fori_loop(0, wc // TILE, expert_grads, 0)
-        cols = pl.ds(c * wc, wc)
-        copy = pltpu.make_async_copy(recv.at[:, cols], eg_hbm.at[:, cols], out_sem.at[c])
-        copy.start()
-        out_copies.append(copy)
+    lane_s = iota((slots, 128), 1)
+    ab = jnp.where(lane_s == 0, alpha, 0.0)
+    ab = jnp.where(lane_s == 1, beta, ab)
+    ab_ref[...] = jnp.where(lane_s == 2, x_code, ab)
 
     for copy in g_copies:
         copy.wait_recv()
@@ -416,6 +411,16 @@
     tg_copy.wait()
     for copy in out_copies:
         copy.wait()
+
+
+def finish(tg_in, x_ref, ghl_ref, ab_ref, tg_ref, eg_ref):
+    tg_ref[...] = tg_in[...]
+    slots, marks = x_ref.shape[0], ghl_ref.shape[0]
+    alpha, beta, code = ab_ref[:, 0:1], ab_ref[:, 1:2], ab_ref[:, 2:3]
+    lane = iota((slots, marks), 1).astype(F32)
+    mark = jnp.where((lane == code) | (lane == code + float(marks // 2)), 1.0, 0.0).astype(BF16)
+    w = dot(mark, ghl_ref[...])
+    eg_ref[...] = (alpha * w - beta * x_ref[...].astype(F32)).astype(BF16)
 
 
 def shards(n_dp, n_ep, tokens, routes, positives, expert_out, router, norm_gain, loss_scale):
@@ -430,7 +435,7 @@
     smem = pl.BlockSpec(memory_space=pltpu.SMEM)
     hbm = pl.BlockSpec(memory_space=pl.ANY)
     router_t = jnp.pad(router.T, ((0, 16 - experts), (0, 0)))
-    token_grad, expert_grad, router_grad, loss = pl.pallas_call(
+    tg_rows, x_rows, router_grad, loss, pooled_hl, factors = pl.pallas_call(
         functools.partial(kernel, n_dp, n_ep, experts, cap),
         name="infonce_step",
         out_shape=(
@@ -438,9 +443,11 @@
             jax.ShapeDtypeStruct((slots, width), BF16),
             jax.ShapeDtypeStruct((n_dp, 8, wr), F32),
             jax.ShapeDtypeStruct((8, 128), F32),
+            jax.ShapeDtypeStruct((4 * ng, width), BF16),
+            jax.ShapeDtypeStruct((slots, 128), F32),
         ),
         in_specs=[hbm, vmem, smem, hbm, vmem, vmem, smem],
-        out_specs=(hbm, hbm, vmem, vmem),
+        out_specs=(hbm, hbm, vmem, vmem, vmem, vmem),
         scratch_shapes=[
             pltpu.VMEM((rows, width), BF16),
             pltpu.VMEM((slots, width), BF16),
@@ -493,6 +500,25 @@
         norm_gain.reshape(1, width),
         loss_scale.reshape(1),
     )
+    tile = min(1024, width)
+    by_cols = lambda n: pl.BlockSpec((n, tile), lambda i: (0, i))
+    token_grad, expert_grad = pl.pallas_call(
+        finish,
+        name="finish_grads",
+        grid=(width // tile,),
+        out_shape=(
+            jax.ShapeDtypeStruct((rows, width), BF16),
+            jax.ShapeDtypeStruct((slots, width), BF16),
+        ),
+        in_specs=[
+            by_cols(rows),
+            by_cols(slots),
+            by_cols(4 * ng),
+            pl.BlockSpec((slots, 128), lambda i: (0, 0)),
+        ],
+        out_specs=(by_cols(rows), by_cols(slots)),
+        compiler_params=pltpu.CompilerParams(vmem_limit_bytes=32 * 1024 * 1024),
+    )(tg_rows, x_rows, pooled_hl, factors)
     router_grad = jnp.transpose(router_grad, (0, 2, 1)).reshape(width, 8)[:, :experts]
     return (token_grad, expert_grad.reshape(expert_out.shape), router_grad, loss[0, 0])
 

time: 135 us -> 137 us (1.015)
  Pallas kernels: 121 us -> 125 us
  local copies, waits for them, and re-layouts: 13 us -> 10.2 us
    pallas_call x0 -> x1, Pallas kernels: none -> 4.34 us  [shards(): pl.pallas_call(finish, name='finish_grads', grid=(width // tile,), out_sh...]
    unnamed x3 -> x11, local copies, waits for them, and re-layouts: 8.84 us -> 6.94 us
where the time goes in v2:
time: 137 us
  Pallas kernels  125 us (91%)
  local copies, waits for them, and re-layouts  10.2 us (7%)
    pallas_call x1, Pallas kernels, shards(): pl.pallas_call(functools.partial(kernel, n_dp, n_ep, experts, cap), name=...  121 us
    unnamed x11, local copies, waits for them, and re-layouts  6.94 us
    pallas_call x1, Pallas kernels, shards(): pl.pallas_call(finish, name='finish_grads', grid=(width // tile,), out_sh...  4.34 us

profile of v2, /device:TPU:0, one launch (start us, length us, event | category | flops | bytes accessed | tf_op | source)
XLA Modules:
  0.0 136.6 jit_solution(10727600341862246715)
XLA Ops:
  1.3 1.4 %copy.11.routes_ref = s32[192,2]{1,0:T(8,128)} copy(s32[192,2]{0,1:T(2,128)} %param.8) | data formatting | bytes 3072 | tf_op args[1]
  2.7 1.4 %pad.4.router_ref = bf16[16,4096]{1,0:T(8,128)(2,1)} pad(bf16[4,4096]{1,0:T(4,128)(2,1)} %bitcast.11, bf16[]{:T(256)} %constant.2.clone.1), padding=0_12x0_0 | pad | bytes 163842 | tf_op jit(solution)/shard_map/jit(_pad)/pad | solution.py:437
  4.2 120.7 %infonce_step.1 = (bf16[192,4096]{1,0:T(8,128)(2,1)}, bf16[512,4096]{1,0:T(8,128)(2,1)}, f32[8,8,512]{2,1,0:T(8,128)}, f32[8,128]{1,0:T(8,128)}, bf16[32,4096]{1,0:T(8,128)(2,1)}, /*index=5*/f32[512,128]{1,0:T(8,128)}) custom-call(bf16[192,4096]{1,0:T(8,128)(2,1)} %tok_hbm.1, s32[192,2]{1,0:T(8,128)} %copy.11.routes_ref, s32[2]{0:T(128)} %pos_ref.1, ...), custom_call_target="tpu_custom_call" | custom-call | tf_op jit(solution)/shard_map/infonce_step/pallas_call | solution.py:438
  124.9 1.2 slice.7
  126.1 0.0 copy-start
  126.1 2.2 %copy-done = bf16[512,4096]{1,0:T(8,128)(2,1)S(1)} copy-done((bf16[512,4096]{1,0:T(8,128)(2,1)S(1)}, bf16[512,4096]{1,0:T(8,128)(2,1)}, u32[]{:S(2)}) %copy-start) | copy-done | bytes 4194328
  128.3 0.0 copy-start.1
  128.3 1.4 %copy-done.1 = bf16[192,4096]{1,0:T(8,128)(2,1)S(1)} copy-done((bf16[192,4096]{1,0:T(8,128)(2,1)S(1)}, bf16[192,4096]{1,0:T(8,128)(2,1)}, u32[]{:S(2)}) %copy-start.1) | copy-done | bytes 1572888
  129.7 0.0 copy-start.2
  129.7 0.9 copy-done.2
  130.6 0.0 copy-start.3
  130.6 0.9 copy-done.3
  131.6 0.0 copy-start.4
  131.6 4.3 %finish_grads.1 = (bf16[192,4096]{1,0:T(8,128)(2,1)}, bf16[512,4096]{1,0:T(8,128)(2,1)}) custom-call(bf16[192,4096]{1,0:T(8,128)(2,1)S(1)} %copy-done.1, bf16[512,4096]{1,0:T(8,128)(2,1)S(1)} %copy-done, bf16[32,4096]{1,0:T(8,128)(2,1)S(1)} %copy-done.2, f32[512,128]{1,0:T(8,128)S(1)} %copy-done.3), custom_call_target="tpu_custom_call" | custom-call | tf_op jit(solution)/shard_map/finish_grads/pallas_call | solution.py:505
  135.9 0.0 copy-done.4
  135.9 0.6 slice.8
Async XLA Ops:
  126.1 2.2 %copy-start = (bf16[512,4096]{1,0:T(8,128)(2,1)S(1)}, bf16[512,4096]{1,0:T(8,128)(2,1)}, u32[]{:S(2)}) copy-start(bf16[512,4096]{1,0:T(8,128)(2,1)} %get-tuple-element.13.x_ref) | copy-start | bytes 12582916
  128.3 1.4 %copy-start.1 = (bf16[192,4096]{1,0:T(8,128)(2,1)S(1)}, bf16[192,4096]{1,0:T(8,128)(2,1)}, u32[]{:S(2)}) copy-start(bf16[192,4096]{1,0:T(8,128)(2,1)} %get-tuple-element.12.tg_in) | copy-start | bytes 4718596
  129.7 0.9 copy-start.2
  130.6 0.9 copy-start.3
  131.6 4.3 %copy-start.4 = (f32[8,8,512]{2,1,0:T(8,128)S(1)}, f32[8,8,512]{2,1,0:T(8,128)}, u32[]{:S(2)}) copy-start(f32[8,8,512]{2,1,0:T(8,128)} %get-tuple-element.18) | copy-start | bytes 393220
